TPU v7x, 32 devices: a whole 2x2x4 slice. The times are simulated.
32 devices in a mesh: row: 8 (over z, x), col: 4 (over y, core).
Axes of the slice: x: 2, y: 2, z: 4, core: 2. Of those that a mesh axis runs over, the one named last changes fastest.
Arguments:
- features: bfloat16 [192, 52, 2048], P('row', 'col'), may hold values from -6 to 6
- crop_rows: int32 [5], replicated, may hold values from 1 to 49, 192 in all
- crop_cols: int32 [5], replicated, may hold values from 25 to 49
- w_point: bfloat16 [2048, 256], P('row'), may hold values from -0.125 to 0.125
- w_atrous: bfloat16 [2048, 27, 256], P('row'), may hold values from -0.046875 to 0.046875
- w_pool: bfloat16 [2048, 256], P('row'), may hold values from -0.125 to 0.125
- w_proj: bfloat16 [1280, 256], P('row'), may hold values from -0.15625 to 0.15625
- gains: float32 [6, 256], replicated, may hold values from 0.5 to 1.5
- biases: float32 [6, 256], replicated, may hold values from -3 to 3
- cotangent: bfloat16 [192, 52, 256], P('row', 'col'), may hold values from -6 to 6
Outputs:
- result: bfloat16 [192, 52, 256], P('row', 'col')
- d_features: bfloat16 [192, 52, 2048], P('row', 'col')
- d_point: float32 [2048, 256], P('row')
- d_atrous: float32 [2048, 27, 256], P('row')
- d_pool: float32 [2048, 256], P('row')
- d_proj: float32 [1280, 256], P('row')
- d_gains: float32 [6, 256], replicated
- d_biases: float32 [6, 256], replicated
Inputs may be any that keep to these rules, and one draw needn't show every extreme that they name: `crop_rows`: crop heights sum to 192; the tallest crop has 49 rows.
All inputs are finite; a program needn't handle non-finite values.
Results may differ from a plain program's by a relative error of at most 0.02.
Values may be sent and summed in bfloat16 or wider, within the bound.
A program may use at most 384 MiB of HBM per device.

v0:
```python
import jax
import jax.numpy as jnp
from jax import lax
from jax.sharding import PartitionSpec as P

EPSILON = 1e-05
MARGIN = 18
DILATIONS = (6, 12, 18)
HIGHEST = lax.Precision.HIGHEST


def padded_2(shard, sides, width):
    for axis, dim in sides:
        devices, length = (lax.axis_size(axis), shard.shape[dim])
        up = [(i, (i + 1) % devices) for i in range(devices - 1)]
        down = [(j, i) for i, j in up]
        last = lax.slice_in_dim(shard, length - width, length, axis=dim)
        first = lax.slice_in_dim(shard, 0, width, axis=dim)
        before = lax.ppermute(last, axis, up)
        after = lax.ppermute(first, axis, down)
        shard = jnp.concatenate([before, shard, after], axis=dim)
    return shard


def silu_slope(values):
    sigma = jax.nn.sigmoid(values)
    return sigma * (1.0 + values * (1.0 - sigma))


def per_device(
    features, crop_rows, crop_cols, w_point, w_atrous, w_pool, w_proj, gains, biases, cotangent
):
    height, breadth, channels = features.shape
    branch_width = gains.shape[1]
    num_crops = crop_rows.shape[0]
    row_pos = lax.axis_index("row")
    col_pos = lax.axis_index("col")
    all_cols = breadth * lax.axis_size("col")
    crop_ends = jnp.cumsum(crop_rows)
    global_rows = row_pos * height - MARGIN + jnp.arange(height + 2 * MARGIN, dtype=jnp.int32)
    crop_extended = jnp.sum((global_rows[:, None] >= crop_ends[None, :]).astype(jnp.int32), axis=1)
    crop_extended = jnp.where(global_rows < 0, -1, crop_extended)
    own_crop = crop_extended[MARGIN : MARGIN + height]
    member = (own_crop[:, None] == jnp.arange(num_crops, dtype=jnp.int32)[None, :]).astype(
        jnp.float32
    )
    widths = jnp.dot(member, crop_cols.astype(jnp.float32), precision=HIGHEST)
    col_global = (col_pos * breadth + jnp.arange(breadth, dtype=jnp.int32)).astype(jnp.float32)
    valid_mask = (col_global[None, :] < widths[:, None]).astype(jnp.float32)
    pixel_mask = valid_mask[:, :, None]
    counts = (crop_rows * crop_cols).astype(jnp.float32)
    pixels = jnp.sum(counts)
    masked = features * pixel_mask.astype(jnp.bfloat16)
    full_point, full_atrous, full_pool, full_proj = (
        lax.all_gather(w_point, "row", axis=0, tiled=True),
        lax.all_gather(w_atrous, "row", axis=0, tiled=True),
        lax.all_gather(w_pool, "row", axis=0, tiled=True),
        lax.all_gather(w_proj, "row", axis=0, tiled=True),
    )
    extended = padded_2(masked, (("row", 0),), MARGIN)
    gathered = lax.all_gather(extended, "col", axis=1, tiled=True)
    padded = jnp.pad(gathered, ((0, 0), (MARGIN, MARGIN), (0, 0)))
    local_sums = jnp.einsum(
        "rk,rcf->kf", member.astype(jnp.bfloat16), masked, preferred_element_type=jnp.float32
    )
    crop_sums = lax.psum(local_sums, ("row", "col"))
    preact = [jnp.einsum("rcf,fo->rco", masked, full_point, preferred_element_type=jnp.float32)]
    for branch_idx, dilation in enumerate(DILATIONS):
        running = jnp.zeros((height, breadth, branch_width), jnp.float32)
        for i in (-1, 0, 1):
            same_crop = (
                crop_extended[MARGIN + i * dilation : MARGIN + i * dilation + height] == own_crop
            ).astype(jnp.float32)
            for j in (-1, 0, 1):
                tap_index = 9 * branch_idx + 3 * (i + 1) + (j + 1)
                window = lax.dynamic_slice(
                    padded,
                    (MARGIN + i * dilation, MARGIN + col_pos * breadth + j * dilation, 0),
                    (height, breadth, channels),
                )
                running = running + same_crop[:, None, None] * jnp.einsum(
                    "rcf,fo->rco",
                    window,
                    full_atrous[:, tap_index, :],
                    preferred_element_type=jnp.float32,
                )
        preact.append(running)
    sum_one = jnp.stack([jnp.sum(value * pixel_mask, axis=(0, 1)) for value in preact])
    sum_two = jnp.stack([jnp.sum(value * value * pixel_mask, axis=(0, 1)) for value in preact])
    sum_one, sum_two = lax.psum((sum_one, sum_two), ("row", "col"))
    centre = sum_one / pixels
    inv_scale = lax.rsqrt(sum_two / pixels - centre * centre + EPSILON)
    normed = [(preact[b] - centre[b]) * inv_scale[b] for b in range(4)]
    activation = [gains[b] * normed[b] + biases[b] for b in range(4)]
    pooled = (crop_sums / counts[:, None]).astype(jnp.bfloat16)
    pool_pre = jnp.dot(pooled, full_pool, preferred_element_type=jnp.float32)
    pool_centre = jnp.mean(pool_pre, axis=0)
    pool_inv = lax.rsqrt(
        jnp.mean(pool_pre * pool_pre, axis=0) - pool_centre * pool_centre + EPSILON
    )
    pool_normed = (pool_pre - pool_centre) * pool_inv
    pool_act = gains[4] * pool_normed + biases[4]
    pool_out = jax.nn.silu(pool_act).astype(jnp.bfloat16)
    pool_pixels = jnp.dot(
        member.astype(jnp.bfloat16), pool_out, preferred_element_type=jnp.float32
    ).astype(jnp.bfloat16)
    joined = jnp.concatenate(
        [jax.nn.silu(value).astype(jnp.bfloat16) for value in activation]
        + [jnp.broadcast_to(pool_pixels[:, None, :], (height, breadth, branch_width))],
        axis=-1,
    )
    projected = jnp.einsum("rch,ho->rco", joined, full_proj, preferred_element_type=jnp.float32)
    proj_one, proj_two = lax.psum(
        (
            jnp.sum(projected * pixel_mask, axis=(0, 1)),
            jnp.sum(projected * projected * pixel_mask, axis=(0, 1)),
        ),
        ("row", "col"),
    )
    proj_centre = proj_one / pixels
    proj_inv = lax.rsqrt(proj_two / pixels - proj_centre * proj_centre + EPSILON)
    proj_normed = (projected - proj_centre) * proj_inv
    proj_act = gains[5] * proj_normed + biases[5]
    result = (jax.nn.silu(proj_act) * pixel_mask).astype(jnp.bfloat16)
    grad_out = cotangent.astype(jnp.float32) * pixel_mask
    grad_act5 = grad_out * silu_slope(proj_act)
    bias_grad5, gain_grad5 = lax.psum(
        (jnp.sum(grad_act5, axis=(0, 1)), jnp.sum(grad_act5 * proj_normed, axis=(0, 1))),
        ("row", "col"),
    )
    grad_pre5 = (
        gains[5]
        * proj_inv
        * (grad_act5 - pixel_mask * (bias_grad5 + proj_normed * gain_grad5) / pixels)
    ).astype(jnp.bfloat16)
    grad_proj = jnp.einsum("rch,rco->ho", joined, grad_pre5, preferred_element_type=jnp.float32)
    grad_joined = jnp.einsum(
        "rco,ho->rch", grad_pre5, full_proj, preferred_element_type=jnp.float32
    )
    grad_acts = [
        grad_joined[:, :, b * branch_width : (b + 1) * branch_width] * silu_slope(activation[b])
        for b in range(4)
    ]
    crop_grad = jnp.einsum(
        "rk,rco->ko", member, grad_joined[:, :, 4 * branch_width :], precision=HIGHEST
    )
    local_bias = jnp.stack([jnp.sum(value, axis=(0, 1)) for value in grad_acts])
    local_gain = jnp.stack([jnp.sum(grad_acts[b] * normed[b], axis=(0, 1)) for b in range(4)])
    bias_grads, gain_grads, crop_grad = lax.psum(
        (local_bias, local_gain, crop_grad), ("row", "col")
    )
    grad_pre = [
        (
            gains[b]
            * inv_scale[b]
            * (grad_acts[b] - pixel_mask * (bias_grads[b] + normed[b] * gain_grads[b]) / pixels)
        ).astype(jnp.bfloat16)
        for b in range(4)
    ]
    pool_grad_act = crop_grad * silu_slope(pool_act)
    bias_grad4 = jnp.sum(pool_grad_act, axis=0)
    gain_grad4 = jnp.sum(pool_grad_act * pool_normed, axis=0)
    grad_pool_pre = (
        gains[4] * pool_inv * (pool_grad_act - (bias_grad4 + pool_normed * gain_grad4) / num_crops)
    ).astype(jnp.bfloat16)
    shard_rows = w_pool.shape[0]
    pooled_shard = lax.dynamic_slice_in_dim(pooled, row_pos * shard_rows, shard_rows, 1)
    grad_pool = lax.dot_general(
        pooled_shard, grad_pool_pre, (((0,), (0,)), ((), ())), preferred_element_type=jnp.float32
    )
    grad_pooled = lax.dot_general(
        grad_pool_pre, full_pool, (((1,), (1,)), ((), ())), preferred_element_type=jnp.float32
    )
    pool_back = jnp.dot(member, grad_pooled / counts[:, None], precision=HIGHEST)
    grad_atrous = jnp.zeros((channels, 27, branch_width), jnp.float32)
    for branch_idx, dilation in enumerate(DILATIONS):
        for i in (-1, 0, 1):
            same_crop = (
                crop_extended[MARGIN + i * dilation : MARGIN + i * dilation + height] == own_crop
            ).astype(jnp.bfloat16)
            for j in (-1, 0, 1):
                tap_index = 9 * branch_idx + 3 * (i + 1) + (j + 1)
                masked_grad = grad_pre[branch_idx + 1] * same_crop[:, None, None]
                corner = (MARGIN + i * dilation, MARGIN + col_pos * breadth + j * dilation, 0)
                window = lax.dynamic_slice(padded, corner, (height, breadth, channels))
                grad_atrous = grad_atrous.at[:, tap_index, :].set(
                    jnp.einsum(
                        "rcf,rco->fo", window, masked_grad, preferred_element_type=jnp.float32
                    )
                )
    grad_point = jnp.einsum("rcf,rco->fo", masked, grad_pre[0], preferred_element_type=jnp.float32)
    local_part = (
        jnp.einsum("rco,fo->rcf", grad_pre[0], full_point, preferred_element_type=jnp.float32)
        + pool_back[:, None, :]
    )
    grad_extended = jnp.zeros((height + 2 * MARGIN, all_cols + 2 * MARGIN, channels), jnp.float32)
    for branch_idx, dilation in enumerate(DILATIONS):
        for i in (-1, 0, 1):
            same_crop = (
                crop_extended[MARGIN + i * dilation : MARGIN + i * dilation + height] == own_crop
            ).astype(jnp.bfloat16)
            for j in (-1, 0, 1):
                tap_index = 9 * branch_idx + 3 * (i + 1) + (j + 1)
                masked_grad = grad_pre[branch_idx + 1] * same_crop[:, None, None]
                corner = (MARGIN + i * dilation, MARGIN + col_pos * breadth + j * dilation, 0)
                current = lax.dynamic_slice(grad_extended, corner, (height, breadth, channels))
                update = jnp.einsum(
                    "rco,fo->rcf",
                    masked_grad,
                    full_atrous[:, tap_index, :],
                    preferred_element_type=jnp.float32,
                )
                grad_extended = lax.dynamic_update_slice(grad_extended, current + update, corner)
    trimmed = grad_extended[:, MARGIN : MARGIN + all_cols, :]
    own_rows = lax.psum_scatter(
        trimmed.astype(jnp.bfloat16), "col", scatter_dimension=1, tiled=True
    ).astype(jnp.float32)
    rim_rows = jnp.concatenate([own_rows[:MARGIN], own_rows[height + MARGIN :]], axis=0)
    returned = padded_2(rim_rows.astype(jnp.bfloat16), (("row", 0),), MARGIN).astype(rim_rows.dtype)
    interior = own_rows[MARGIN : MARGIN + height] + local_part
    interior = interior.at[:MARGIN].add(returned[:MARGIN])
    interior = interior.at[height - MARGIN :].add(returned[3 * MARGIN :])
    d_features = (interior * pixel_mask).astype(jnp.bfloat16)
    summed_point, summed_atrous, summed_proj = (
        lax.psum(grad_point.astype(jnp.bfloat16), "col").astype(jnp.float32),
        lax.psum(grad_atrous.astype(jnp.bfloat16), "col").astype(jnp.float32),
        lax.psum(grad_proj.astype(jnp.bfloat16), "col").astype(jnp.float32),
    )
    shard_point, shard_atrous, shard_proj = (
        lax.psum_scatter(summed_point, "row", scatter_dimension=0, tiled=True),
        lax.psum_scatter(summed_atrous, "row", scatter_dimension=0, tiled=True),
        lax.psum_scatter(summed_proj, "row", scatter_dimension=0, tiled=True),
    )
    d_gains = jnp.concatenate([gain_grads, gain_grad4[None, :], gain_grad5[None, :]], axis=0)
    d_biases = jnp.concatenate([bias_grads, bias_grad4[None, :], bias_grad5[None, :]], axis=0)
    return (result, d_features, shard_point, shard_atrous, grad_pool, shard_proj, d_gains, d_biases)


def solution(mesh):
    return jax.shard_map(
        per_device,
        mesh=mesh,
        in_specs=(
            P("row", "col", None),
            P(),
            P(),
            P("row", None),
            P("row", None, None),
            P("row", None),
            P("row", None),
            P(),
            P(),
            P("row", "col", None),
        ),
        out_specs=(
            P("row", "col", None),
            P("row", "col", None),
            P("row", None),
            P("row", None, None),
            P("row", None),
            P("row", None),
            P(),
            P(),
        ),
        check_vma=False,
    )
```

profile of v0, /device:TPU:9, one launch (start us, length us, event | category | flops | bytes accessed | tf_op | source)
XLA Modules:
  0.0 2655.4 jit_solution(7808559889719613198)
XLA Ops:
  18.7 53.6 %collective-permute-done = bf16[18,13,2048]{2,1,0:T(8,128)(2,1)S(1)} collective-permute-done((bf16[18,13,2048]{2,1,0:T(8,128)(2,1)S(1)}, bf16[18,13,2048]{2,1,0:T(8,128)(2,1)S(1)}, u32[]{:S(2)}, u32[]{:S(2)}) %collective-permute-start) | collective-permute-done | bytes 958496 | tf_op jit(solution)/shard_map/ppermute | solution.py:19
  76.4 3.6 copy.133
  84.4 26.2 all_gather.19
  112.7 57.5 %all-gather.7.cloned.1.call-done = bf16[60,52,2048]{2,0,1:T(8,128)(2,1)} async-done(((bf16[60,13,2048]{2,0,1:T(8,128)(2,1)}), bf16[60,52,2048]{2,0,1:T(8,128)(2,1)}) %all-gather.7.cloned.1.call-update) | async-done | bytes 12779536 | tf_op jit(solution)/shard_map/all_gather | solution.py:61
  172.3 538.7 %all-gather.9.cloned.1.call-done = bf16[2048,27,256]{2,0,1:T(8,128)(2,1)} async-done(((bf16[256,27,256]{2,0,1:T(8,128)(2,1)}), bf16[2048,27,256]{2,0,1:T(8,128)(2,1)}) %all-gather.9.cloned.1.call-update) | async-done | bytes 28311568 | tf_op jit(solution)/shard_map/all_gather | solution.py:56
  721.2 5.4 copy-done.1
  743.6 39.1 %all-reduce.5 = (f32[4,256]{1,0:T(4,128)S(1)}, f32[4,256]{1,0:T(4,128)S(1)}, f32[5,2048]{1,0:T(8,128)S(1)}) all-reduce(f32[4,256]{1,0:T(4,128)S(1)} %get-tuple-element.485, f32[4,256]{1,0:T(4,128)S(1)} %get-tuple-element.484, f32[5,2048]{1,0:T(8,128)S(1)} %fusion.65), channel_id=1, replica_groups=mesh['row'=8,'col'=4] {'row','col'}, use_global_device_ids=true, to_apply=%region_12.13 | all-reduce | flops 12288 | bytes 98304 | tf_op jit(solution)/shard_map/psum | solution.py:90
  788.9 40.1 %all-reduce.4 = (f32[256]{0:T(256)S(1)}, f32[256]{0:T(256)S(1)}) all-reduce(f32[256]{0:T(256)S(1)} %get-tuple-element.369, f32[256]{0:T(256)S(1)} %get-tuple-element.368), channel_id=1, replica_groups=mesh['row'=8,'col'=4] {'row','col'}, use_global_device_ids=true, to_apply=%region_18.19 | all-reduce | flops 512 | bytes 4096 | tf_op jit(solution)/shard_map/psum | solution.py:113
  830.6 40.0 %all-reduce.3 = (f32[256]{0:T(256)S(1)}, f32[256]{0:T(256)S(1)}) all-reduce(f32[256]{0:T(256)S(1)} %get-tuple-element.365, f32[256]{0:T(256)S(1)} %get-tuple-element.364), channel_id=1, replica_groups=mesh['row'=8,'col'=4] {'row','col'}, use_global_device_ids=true, to_apply=%region_24.25 | all-reduce | flops 512 | bytes 4096 | tf_op jit(solution)/shard_map/psum | solution.py:127
  879.0 40.9 %all-reduce.2 = (f32[4,256]{1,0:T(4,128)S(1)}, f32[4,256]{1,0:T(4,128)S(1)}, f32[5,256]{1,0:T(8,128)}) all-reduce(f32[4,256]{1,0:T(4,128)S(1)} %pad_maximum_fusion.9, f32[4,256]{1,0:T(4,128)S(1)} %pad_maximum_fusion.8, f32[5,256]{1,0:T(8,128)S(1)} %fusion.64), channel_id=1, replica_groups=mesh['row'=8,'col'=4] {'row','col'}, use_global_device_ids=true, to_apply=%region_34.35 | all-reduce | flops 3328 | bytes 26624 | tf_op jit(solution)/shard_map/psum | solution.py:149
  924.2 11.4 scatter.90
  989.1 16.5 broadcast_in_dim.18
  1005.6 10.3 dynamic_update_slice.81
  1018.7 10.3 dynamic_update_slice.82
  1031.9 10.3 dynamic_update_slice.83
  1045.5 10.5 dynamic_update_slice.84
  1058.7 10.3 dynamic_update_slice.85
  1071.9 10.3 dynamic_update_slice.86
  1082.2 4.1 fusion.6
  1086.3 4.1 fusion.5
  1090.4 4.2 fusion.4
  1097.6 10.4 dynamic_update_slice.90
  1111.2 10.5 dynamic_update_slice.91
  1124.6 10.3 dynamic_update_slice.92
  1137.7 10.3 dynamic_update_slice.93
  1150.8 10.3 dynamic_update_slice.94
  1164.0 10.6 dynamic_update_slice.95
  1177.4 10.2 dynamic_update_slice.96
  1190.6 10.1 dynamic_update_slice.97
  1203.7 10.3 dynamic_update_slice.98
  1213.9 4.1 fusion.3
  1218.0 4.1 fusion.2
  1222.1 4.1 fusion.1
  1229.0 10.3 dynamic_update_slice.102
  1242.2 10.6 dynamic_update_slice.103
  1255.7 10.3 dynamic_update_slice.104
  1268.8 10.0 dynamic_update_slice.105
  1281.7 9.9 dynamic_update_slice.106
  1294.5 10.1 dynamic_update_slice.107
  1304.5 15.6 slice.1146
  1320.2 171.0 %all-reduce.9.cloned.1.call-done = (bf16[2048,256]{1,0:T(8,128)(2,1)}, bf16[2048,27,256]{2,0,1:T(8,128)(2,1)}, bf16[1280,256]{1,0:T(8,128)(2,1)}) async-done(((bf16[2048,256]{1,0:T(8,128)(2,1)}, bf16[2048,27,256]{2,0,1:T(8,128)(2,1)}, bf16[1280,256]{1,0:T(8,128)(2,1)}), (bf16[2048,256]{1,0:T(8,128)(2,1)}, bf16[2048,27,256]{2,0,1:T(8,128)(2,1)}, bf16[1280,256]{1,0:T(8,128)(2,1)})) %all-reduce.9.cloned.1.call-update) | async-done | bytes 30015504 | tf_op jit(solution)/shard_map/psum | solution.py:225
  1496.3 30.8 %convert_element_type.212 = f32[2048,27,256]{2,0,1:T(8,128)} convert(bf16[2048,27,256]{2,0,1:T(8,128)(2,1)} %get-tuple-element.405) | non-fusion elementwise | flops 14155776 | bytes 84934656 | tf_op jit(solution)/shard_map/convert_element_type | solution.py:226
  1528.8 71.6 %reduce-scatter.5.cloned.1.call-done = bf16[60,13,2048]{2,0,1:T(8,128)(2,1)} async-done(((bf16[60,52,2048]{2,0,1:T(8,128)(2,1)}), bf16[60,13,2048]{2,0,1:T(8,128)(2,1)}) %reduce-scatter.5.cloned.1.call-update) | async-done | bytes 3194896 | tf_op jit(solution)/shard_map/reduce_scatter | solution.py:215
  1615.4 45.7 %collective-permute-done.2 = bf16[18,13,2048]{2,1,0:T(8,128)(2,1)S(1)} collective-permute-done((bf16[18,13,2048]{2,1,0:T(8,128)(2,1)S(1)}, bf16[18,13,2048]{2,1,0:T(8,128)(2,1)S(1)}, u32[]{:S(2)}, u32[]{:S(2)}) %collective-permute-start.2) | collective-permute-done | bytes 958496 | tf_op jit(solution)/shard_map/ppermute | solution.py:19
  1667.9 10.9 scatter-add.6
  1682.3 11.0 scatter-add.9
  1694.5 67.5 %reduce-scatter.7.cloned.1.call-done = f32[256,256]{1,0:T(8,128)} async-done(((f32[2048,256]{1,0:T(8,128)}), f32[256,256]{1,0:T(8,128)}) %reduce-scatter.7.cloned.1.call-update) | async-done | bytes 262160 | tf_op jit(solution)/shard_map/reduce_scatter | solution.py:230
  1762.0 886.7 %reduce-scatter.9.cloned.1.call-done = f32[256,27,256]{2,0,1:T(8,128)} async-done(((f32[2048,27,256]{2,0,1:T(8,128)}), f32[256,27,256]{2,0,1:T(8,128)}) %reduce-scatter.9.cloned.1.call-update) | async-done | bytes 7077904 | tf_op jit(solution)/shard_map/reduce_scatter | solution.py:231
  (289 shorter events, 215.7 us)
Async XLA Ops:
  7.2 103.4 %all-gather.5.cloned.1.call-start = ((), (), s32[]{:S(2)}) async-start(), calls=%async_computation.4 | async-start | bytes 1179648 | tf_op jit(solution)/shard_map/all_gather | solution.py:55
  7.9 162.4 %all-gather.7.cloned.1.call-start = ((), (), s32[]{:S(2)}) async-start(), calls=%async_computation.5 | async-start | bytes 17039360 | tf_op jit(solution)/shard_map/all_gather | solution.py:61
  9.0 869.7 %copy-start.46 = (s32[24]{0:T(128)}, s32[24]{0:T(128)S(1)}, u32[]{:S(2)}) copy-start(s32[24]{0:T(128)S(1)} %slice.880) | copy-start | bytes 292
  9.9 933.2 %copy-start.13 = (f32[24,13]{0,1:T(8,128)}, f32[24,13]{0,1:T(8,128)S(1)}, u32[]{:S(2)}) copy-start(f32[24,13]{0,1:T(8,128)S(1)} %get-tuple-element.467) | copy-start | bytes 3748
  10.0 100.6 %copy-start.20 = (bf16[24,13]{1,0:T(8,128)(2,1)}, bf16[24,13]{1,0:T(8,128)(2,1)S(1)}, u32[]{:S(2)}) copy-start(bf16[24,13]{1,0:T(8,128)(2,1)S(1)} %copy.130) | copy-start | bytes 1876
  12.1 70.1 %copy-start.6 = (bf16[24,13,2048]{2,0,1:T(8,128)(2,1)S(1)}, bf16[24,13,2048]{2,0,1:T(8,128)(2,1)}, u32[]{:S(2)}) copy-start(bf16[24,13,2048]{2,0,1:T(8,128)(2,1)} %param.68) | copy-start | bytes 3833860
  12.1 71.3 %copy-start.52 = (s32[5]{0:T(128)S(1)}, s32[5]{0:T(128)}, u32[]{:S(2)}) copy-start(s32[5]{0:T(128)} %param.69) | copy-start | bytes 64
  12.1 71.3 %copy-start.53 = (s32[5]{0:T(128)S(1)}, s32[5]{0:T(128)}, u32[]{:S(2)}) copy-start(s32[5]{0:T(128)} %param.70) | copy-start | bytes 64
  12.1 72.2 %copy-start.40 = (f32[6,256]{1,0:T(8,128)S(1)}, f32[6,256]{1,0:T(8,128)}, u32[]{:S(2)}) copy-start(f32[6,256]{1,0:T(8,128)} %param.76) | copy-start | bytes 18436
  12.1 72.2 %copy-start.17 = (bf16[160,256]{1,0:T(8,128)(2,1)S(1)}, bf16[160,256]{1,0:T(8,128)(2,1)}, u32[]{:S(2)}) copy-start(bf16[160,256]{1,0:T(8,128)(2,1)} %param.74) | copy-start | bytes 245764
  12.5 59.8 %collective-permute-start = (bf16[18,13,2048]{2,1,0:T(8,128)(2,1)S(1)}, bf16[18,13,2048]{2,1,0:T(8,128)(2,1)S(1)}, u32[]{:S(2)}, u32[]{:S(2)}) collective-permute-start(bf16[18,13,2048]{2,1,0:T(8,128)(2,1)S(1)} %get-tuple-element.427), channel_id=1, source_target_pairs={{0,4},{4,8},{8,12},{12,16},{16,20},{20,24},{24,28},{1,5},{5,9},{9,... | collective-permute-start | bytes 2875400 | tf_op jit(solution)/shard_map/ppermute | solution.py:19
  15.6 59.9 %collective-permute-start.1 = (bf16[18,13,2048]{2,1,0:T(8,128)(2,1)S(1)}, bf16[18,13,2048]{2,1,0:T(8,128)(2,1)S(1)}, u32[]{:S(2)}, u32[]{:S(2)}) collective-permute-start(bf16[18,13,2048]{2,1,0:T(8,128)(2,1)S(1)} %get-tuple-element.428), channel_id=1, source_target_pairs={{4,0},{8,4},{12,8},{16,12},{20,16},{24,20},{28,24},{5,1},{9,5},{13... | collective-permute-start | bytes 2875400 | tf_op jit(solution)/shard_map/ppermute | solution.py:20
  80.1 631.0 %all-gather.9.cloned.1.call-start = ((), (), s32[]{:S(2)}) async-start(), calls=%async_computation.6 | async-start | bytes 31850496 | tf_op jit(solution)/shard_map/all_gather | solution.py:56
  80.8 702.7 %all-gather.11.cloned.1.call-start = ((), (), s32[]{:S(2)}) async-start(), calls=%async_computation.7 | async-start | bytes 1179648 | tf_op jit(solution)/shard_map/all_gather | solution.py:57
  81.4 1409.8 %all-reduce.9.cloned.1.call-start = ((), (), s32[]{:S(2)}) async-start(), calls=%async_computation.12 | async-start | bytes 60030976 | tf_op jit(solution)/shard_map/psum | solution.py:225
  84.1 699.3 %copy-start.37 = (f32[5]{0:T(128)}, f32[5]{0:T(128)S(1)}, u32[]{:S(2)}) copy-start(f32[5]{0:T(128)S(1)} %get-tuple-element.416) | copy-start | bytes 64
  84.4 701.8 %copy-start.44 = (f32[1,256]{1,0:T(1,128)}, f32[1,256]{1,0:T(1,128)S(1)}, u32[]{:S(2)}) copy-start(f32[1,256]{1,0:T(1,128)S(1)} %get-tuple-element.446) | copy-start | bytes 3076
  711.0 5.7 copy-start
  716.7 9.9 copy-start.1
  741.7 43.3 %copy-start.39 = (f32[6,256]{1,0:T(8,128)S(1)}, f32[6,256]{1,0:T(8,128)}, u32[]{:S(2)}) copy-start(f32[6,256]{1,0:T(8,128)} %param.75) | copy-start | bytes 18436
  742.5 87.2 %copy-start.15 = (bf16[24,13,256]{2,0,1:T(8,128)(2,1)S(1)}, bf16[24,13,256]{2,0,1:T(8,128)(2,1)}, u32[]{:S(2)}) copy-start(bf16[24,13,256]{2,0,1:T(8,128)(2,1)} %param.77) | copy-start | bytes 479236
  870.5 53.6 %copy-start.48 = (f32[256]{0:T(256)}, f32[256]{0:T(256)S(1)}, u32[]{:S(2)}) copy-start(f32[256]{0:T(256)S(1)} %get-tuple-element.398) | copy-start | bytes 3076
  870.5 53.6 %copy-start.50 = (f32[256]{0:T(256)}, f32[256]{0:T(256)S(1)}, u32[]{:S(2)}) copy-start(f32[256]{0:T(256)S(1)} %get-tuple-element.397) | copy-start | bytes 3076
  919.8 15.8 copy-start.30
  919.8 15.8 copy-start.32
  921.7 13.9 slice-start
  921.7 13.9 slice-start.1
  924.2 11.4 slice-start.2
  924.2 11.4 slice-start.3
  941.4 4.7 copy-start.27
  944.1 33.5 %copy-start.11 = (bf16[24,13,256]{2,0,1:T(8,128)(2,1)}, bf16[24,13,256]{2,0,1:T(8,128)(2,1)S(1)}, u32[]{:S(2)}) copy-start(bf16[24,13,256]{2,0,1:T(8,128)(2,1)S(1)} %get-tuple-element.440) | copy-start | bytes 479236
  964.7 3.8 copy-start.24
  973.9 3.7 copy-start.21
  987.3 613.1 %reduce-scatter.5.cloned.1.call-start = ((), (), s32[]{:S(2)}) async-start(), calls=%async_computation.8 | async-start | bytes 17039360 | tf_op jit(solution)/shard_map/reduce_scatter | solution.py:215
  1320.2 374.4 %reduce-scatter.11.cloned.1.call-start = ((), (), s32[]{:S(2)}) async-start(), calls=%async_computation.11 | async-start | bytes 1474560 | tf_op jit(solution)/shard_map/reduce_scatter | solution.py:232
  1493.5 268.5 %reduce-scatter.7.cloned.1.call-start = ((), (), s32[]{:S(2)}) async-start(), calls=%async_computation.9 | async-start | bytes 2359296 | tf_op jit(solution)/shard_map/reduce_scatter | solution.py:230
  1496.3 1152.4 %reduce-scatter.9.cloned.1.call-start = ((), (), s32[]{:S(2)}) async-start(), calls=%async_computation.10 | async-start | bytes 63700992 | tf_op jit(solution)/shard_map/reduce_scatter | solution.py:231
  1527.2 82.6 %copy-start.33 = (f32[4,256]{1,0:T(4,128)S(1)}, f32[4,256]{1,0:T(4,128)}, u32[]{:S(2)}) copy-start(f32[4,256]{1,0:T(4,128)} %copy-done.32) | copy-start | bytes 12292
  1527.2 82.6 %copy-start.51 = (f32[256]{0:T(256)S(1)}, f32[256]{0:T(256)}, u32[]{:S(2)}) copy-start(f32[256]{0:T(256)} %copy-done.50) | copy-start | bytes 3076
  1527.2 83.2 %copy-start.31 = (f32[4,256]{1,0:T(4,128)S(1)}, f32[4,256]{1,0:T(4,128)}, u32[]{:S(2)}) copy-start(f32[4,256]{1,0:T(4,128)} %copy-done.30) | copy-start | bytes 12292
  1527.2 83.2 %copy-start.49 = (f32[256]{0:T(256)S(1)}, f32[256]{0:T(256)}, u32[]{:S(2)}) copy-start(f32[256]{0:T(256)} %copy-done.48) | copy-start | bytes 3076
  1527.2 83.8 %copy-start.47 = (s32[24]{0:T(128)S(1)}, s32[24]{0:T(128)}, u32[]{:S(2)}) copy-start(s32[24]{0:T(128)} %copy-done.46) | copy-start | bytes 292
  1527.2 85.7 %copy-start.12 = (bf16[24,13,256]{2,0,1:T(8,128)(2,1)S(1)}, bf16[24,13,256]{2,0,1:T(8,128)(2,1)}, u32[]{:S(2)}) copy-start(bf16[24,13,256]{2,0,1:T(8,128)(2,1)} %copy-done.11) | copy-start | bytes 479236
  1602.5 62.4 %copy-start.2 = (bf16[18,13,2048]{2,0,1:T(8,128)(2,1)}, bf16[18,13,2048]{2,0,1:T(8,128)(2,1)S(1)}, u32[]{:S(2)}) copy-start(bf16[18,13,2048]{2,0,1:T(8,128)(2,1)S(1)} %get-tuple-element.417) | copy-start | bytes 2875396
  1602.5 62.4 %copy-start.3 = (bf16[18,13,2048]{2,0,1:T(8,128)(2,1)}, bf16[18,13,2048]{2,0,1:T(8,128)(2,1)S(1)}, u32[]{:S(2)}) copy-start(bf16[18,13,2048]{2,0,1:T(8,128)(2,1)S(1)} %get-tuple-element.418) | copy-start | bytes 2875396
  1603.1 58.0 %collective-permute-start.2 = (bf16[18,13,2048]{2,1,0:T(8,128)(2,1)S(1)}, bf16[18,13,2048]{2,1,0:T(8,128)(2,1)S(1)}, u32[]{:S(2)}, u32[]{:S(2)}) collective-permute-start(bf16[18,13,2048]{2,1,0:T(8,128)(2,1)S(1)} %copy.142), channel_id=1, source_target_pairs={{0,4},{4,8},{8,12},{12,16},{16,20},{20,24},{24,28},{1,5},{5,9},{9,... | collective-permute-start | bytes 2875400 | tf_op jit(solution)/shard_map/ppermute | solution.py:19
  1606.7 57.6 %collective-permute-start.3 = (bf16[18,13,2048]{2,1,0:T(8,128)(2,1)S(1)}, bf16[18,13,2048]{2,1,0:T(8,128)(2,1)S(1)}, u32[]{:S(2)}, u32[]{:S(2)}) collective-permute-start(bf16[18,13,2048]{2,1,0:T(8,128)(2,1)S(1)} %copy.143), channel_id=1, source_target_pairs={{4,0},{8,4},{12,8},{16,12},{20,16},{24,20},{28,24},{5,1},{9,5},{13... | collective-permute-start | bytes 2875400 | tf_op jit(solution)/shard_map/ppermute | solution.py:20
  1666.0 27.3 %copy-start.14 = (f32[24,13]{0,1:T(8,128)S(1)}, f32[24,13]{0,1:T(8,128)}, u32[]{:S(2)}) copy-start(f32[24,13]{0,1:T(8,128)} %copy-done.13) | copy-start | bytes 3748
  (23 other events, 40.7 us)
Sparse Core Ops, SparseCore 0:
  10.1 70.8 all-gather.4
  83.1 87.1 all-gather.6
  171.8 539.1 all-gather.8
  713.0 38.2 all-gather.10
  987.4 503.7 all-reduce.8
  1493.8 106.4 reduce-scatter.4
  1604.7 85.8 reduce-scatter.10
  1695.1 66.8 reduce-scatter.6
  1767.1 881.5 reduce-scatter.8
where the time goes:
time: 2670 us; the launch traced here: 2660 us
  waiting for transfers between devices  1900 us (71%)
  local copies, waits for them, and re-layouts  304 us (11%)
  blocking collectives  186 us (7%)
  matrix products  178 us (7%)
  other arithmetic  59 us (2%)
    reduce_scatter x1, waiting for transfers between devices, per_device(): lax.psum_scatter(summed_atrous, 'row', scatter_dimension=0, tiled=True)  887 us
    all_gather x1, waiting for transfers between devices, per_device(): lax.all_gather(w_atrous, 'row', axis=0, tiled=True)  539 us
    dynamic_update_slice x21, local copies, waits for them, and re-layouts, per_device(): lax.dynamic_update_slice(grad_extended, current + update, corner)  216 us
    psum x1, waiting for transfers between devices, per_device(): lax.psum(grad_point.astype(jnp.bfloat16), 'col').astype(jnp.float32)  171 us
    ppermute x2, waiting for transfers between devices, padded_2(): before = lax.ppermute(last, axis, up)  99.4 us
    dot_general x27, matrix products, per_device(): jnp.einsum('rco,fo->rcf', masked_grad, full_atrous[:, tap_index, :], pref...  84.5 us
    reduce_scatter x1, waiting for transfers between devices, per_device(): lax.psum_scatter(trimmed.astype(jnp.bfloat16), 'col', scatter_dimension=1...  71.6 us
    reduce_scatter x1, waiting for transfers between devices, per_device(): lax.psum_scatter(summed_point, 'row', scatter_dimension=0, tiled=True)  67.5 us
  transfers between devices with their start and end apart: 13, of which 10 were waited for; matrix products, arithmetic and copies ran while one was open for 17% of the time, Pallas kernels for 0%

commit v1 on v0

v1 whole, which is shorter than its diff:
```python
import functools

import jax
import jax.numpy as jnp
import numpy as np
from jax import lax
from jax.experimental import pallas as pl
from jax.experimental.pallas import tpu as pltpu
from jax.sharding import PartitionSpec as P

EPSILON = 1e-05
MARGIN = 18
DILATIONS = (6, 12, 18)
MEMBERS = 8
TAPS = 29
MESH = pl.DeviceIdType.MESH
F32 = jnp.float32
BF16 = jnp.bfloat16
GROUPS = ((0, 4), (4, 7), (7, 10), (10, 13), (13, 16), (16, 19), (19, 22), (22, 25), (25, 29))


def up_to(value, multiple):
    return -(-value // multiple) * multiple


class Plan:
    def __init__(self, rows_axis, cols_axis, h, bc, channels, width, crops):
        self.R, self.C = rows_axis, cols_axis
        self.h, self.bc, self.channels, self.width = h, bc, channels, width
        self.G = MEMBERS // self.C
        self.slabs = self.R // self.G
        self.H = self.G * h
        self.cols = bc * self.C
        self.S = up_to(self.cols, 8)
        self.rpb = self.H // MEMBERS
        self.px = self.rpb * self.S
        self.own = MEMBERS * self.px
        self.hb = MARGIN // self.rpb
        self.nb = MEMBERS + 2 * self.hb
        self.ext = self.nb * self.px
        self.bp = up_to(bc, 16)
        self.cs = channels // MEMBERS
        self.part = self.cs // self.C
        self.crops = crops
        self.ncp = up_to(crops, 16)
        self.exchange = self.slabs == self.C and self.R == MEMBERS
        self.steps = tuple(d // self.rpb for d in DILATIONS)


def remote(src, dst, send, recv, device):
    return pltpu.make_async_remote_copy(
        src_ref=src, dst_ref=dst, send_sem=send, recv_sem=recv, device_id=device, device_id_type=MESH
    )


def greet_all(pn, row, col):
    total = pn.R * pn.C
    barrier = pltpu.get_barrier_semaphore()
    me = row * pn.C + col

    def hello(k, carry):
        other = lax.rem(me + k, total)
        pl.semaphore_signal(
            barrier, inc=1, device_id=(other // pn.C, lax.rem(other, pn.C)), device_id_type=MESH
        )
        return carry

    lax.fori_loop(1, total, hello, 0)
    pl.semaphore_wait(barrier, total - 1)


def dot(a, b):
    return jnp.dot(a, b, preferred_element_type=F32)


def dot_nt(a, b):
    return lax.dot_general(a, b, (((1,), (1,)), ((), ())), preferred_element_type=F32)


def dot_tn(a, b):
    return lax.dot_general(a, b, (((0,), (0,)), ((), ())), preferred_element_type=F32)


def split_dot(dot_fn, a, b):
    high = a.astype(BF16)
    low = (a - high.astype(F32)).astype(BF16)
    return dot_fn(high, b) + dot_fn(low, b)


def conv_kernel(pn, feats, w_in, cot, masks, sel, hot_t, inv_counts, p_out, x_out, w_out, m_out, p4_out, cot_out,
                ring, xs, wbuf, acc, pbuf, cbuf, sbuf, rbuf, cx,
                f_s, f_r, h_s, h_up, h_dn, c_s, c_r, w_s, w_r, w_l, r1_s, r1_r, r2_s, r2_r, o_s):
    row, col = lax.axis_index("row"), lax.axis_index("col")
    slab, x = row // pn.G, lax.rem(row, pn.G)
    me = x * pn.C + col
    core, quad = lax.rem(col, 2), me // 2
    h, H, bp, px = pn.h, pn.H, pn.bp, pn.px

    def member(s, k):
        return (s * pn.G + k // pn.C, lax.rem(k, pn.C))

    greet_all(pn, row, col)

    own_cols = pl.ds(pl.multiple_of(col * bp, bp), bp)
    own_rows = pl.ds(MARGIN + h * x, h)
    sent = []
    for kk in range(1, MEMBERS):
        other = lax.rem(me + kk, MEMBERS)
        c = remote(feats.at[other], ring.at[own_rows, own_cols], f_s.at[kk], f_r.at[kk], member(slab, other))
        c.start()
        sent.append(c)
    keep = pltpu.make_async_copy(feats.at[me], ring.at[own_rows, own_cols], f_r.at[0])
    keep.start()
    to_up, to_down = (x == 0) & (slab > 0), (x == pn.G - 1) & (slab < pn.slabs - 1)

    def halo(kk, down):
        if down:
            src, dst, sem, s = feats.at[kk, pl.ds(h - MARGIN, MARGIN)], ring.at[pl.ds(0, MARGIN), own_cols], h_up, slab + 1
        else:
            src, dst, sem, s = feats.at[kk, pl.ds(0, MARGIN)], ring.at[pl.ds(MARGIN + H, MARGIN), own_cols], h_dn, slab - 1
        return remote(src, dst, h_s.at[int(down), kk], sem.at[col], (s * pn.G + kk // pn.C, kk % pn.C))

    @pl.when(to_up)
    def _():
        for kk in range(MEMBERS):
            halo(kk, False).start()

    @pl.when(to_down)
    def _():
        for kk in range(MEMBERS):
            halo(kk, True).start()

    cot_sent = []
    for cc in range(1, pn.C):
        cd = lax.rem(col + cc, pn.C)
        c = remote(cot.at[pl.ds(cd * pn.rpb, pn.rpb)], cx.at[:, own_cols], c_s.at[cc], c_r.at[cc], (row, cd))
        c.start()
        cot_sent.append(c)
    cot_keep = pltpu.make_async_copy(cot.at[pl.ds(col * pn.rpb, pn.rpb)], cx.at[:, own_cols], c_r.at[0])
    cot_keep.start()

    def w_local(g):
        a, b = GROUPS[g]
        return pltpu.make_async_copy(w_in.at[pl.ds(a, b - a)], wbuf.at[pl.ds(a, b - a)], w_l.at[g])

    def w_send(g, zz, src_col):
        a, b = GROUPS[g]
        to = lax.rem(slab + zz, pn.slabs)
        rows = pl.ds(pl.multiple_of(src_col * pn.part, pn.part), pn.part)
        return remote(w_in.at[pl.ds(a, b - a), rows], wbuf.at[pl.ds(a, b - a), rows],
                      w_s.at[zz, g], w_r.at[g, src_col], (to * pn.G + x, slab))

    if pn.exchange:
        for g in range(len(GROUPS)):
            for zz in range(1, pn.slabs):
                w_send(g, zz, col).start()

        @pl.when(slab == col)
        def _():
            for g in range(len(GROUPS)):
                w_local(g).start()
    else:
        for g in range(len(GROUPS)):
            w_local(g).start()

    def w_wait(g):
        if pn.exchange:
            @pl.when(slab == col)
            def _():
                w_local(g).wait()

            @pl.when(slab != col)
            def _():
                for j in range(pn.C):
                    w_send(g, 1, j).wait_recv()
        else:
            w_local(g).wait()

    @pl.when(slab == 0)
    def _():
        ring[pl.ds(0, MARGIN)] = jnp.zeros((MARGIN, pn.C * bp, pn.cs), BF16)

    @pl.when(slab == pn.slabs - 1)
    def _():
        ring[pl.ds(MARGIN + H, MARGIN)] = jnp.zeros((MARGIN, pn.C * bp, pn.cs), BF16)

    for c in sent:
        c.wait()
    keep.wait()

    @pl.when(slab > 0)
    def _():
        for j in range(pn.C):
            remote(feats.at[0, pl.ds(0, MARGIN)], ring.at[pl.ds(0, MARGIN), pl.ds(j * bp, bp)], h_s.at[0, 0], h_up.at[j],
                   member(slab - 1, me)).wait_recv()

    @pl.when(slab < pn.slabs - 1)
    def _():
        for j in range(pn.C):
            remote(feats.at[0, pl.ds(0, MARGIN)], ring.at[pl.ds(MARGIN + H, MARGIN), pl.ds(j * bp, bp)], h_s.at[0, 0],
                   h_dn.at[j], member(slab + 1, me)).wait_recv()

    def assemble(rp, carry):
        pair = ring[pl.ds(2 * rp, 2)].reshape(2 * pn.C * bp, pn.cs)
        moved = dot(sel[...], pair).astype(BF16)
        at = pl.multiple_of(rp * 2 * pn.S, 16)
        for v in range(7):
            xs[v, pl.ds(at, 2 * pn.S)] = moved[v * 2 * pn.S:(v + 1) * 2 * pn.S]
        return carry

    lax.fori_loop(0, pn.nb * pn.rpb // 2, assemble, 0)
    x_save = pltpu.make_async_copy(xs, x_out, o_s.at[0])
    x_save.start()

    for c in cot_sent:
        c.wait()
    cot_keep.wait()
    for rp in range(pn.rpb // 2):
        pair = cx[2 * rp:2 * rp + 2].reshape(2 * pn.C * bp, pn.width)
        cot_out[pl.ds(rp * 2 * pn.S, 2 * pn.S)] = dot(sel[pl.ds(3 * 2 * pn.S, 2 * pn.S)], pair).astype(BF16)

    def first_stage(slot):
        return remote(pbuf.at[slot, :, 1 - core], cbuf.at[slot], r1_s.at[slot], r1_r.at[slot], (row, col + 1 - 2 * core))

    def second_stage(slot, i):
        q = lax.rem(quad + i, MEMBERS // 2)
        return remote(sbuf.at[slot, i - 1], rbuf.at[slot, i - 1], r2_s.at[slot, i - 1], r2_r.at[slot, i - 1],
                      member(slab, 2 * q + core))

    def middle(slot):
        first_stage(slot).wait()
        for i in range(MEMBERS // 2):
            q = lax.rem(quad + i, MEMBERS // 2)
            s = pbuf[slot, q, core].astype(F32) + cbuf[slot, q].astype(F32)
            if i == 0:
                p_out[slot] = s
            else:
                sbuf[slot, i - 1] = s.astype(BF16)
                second_stage(slot, i).start()

    def last(slot):
        total = p_out[slot]
        for i in range(1, MEMBERS // 2):
            second_stage(slot, i).wait()
            total = total + rbuf[slot, i - 1].astype(F32)
        p_out[slot] = total

    for branch in (1, 2, 3):
        step = pn.steps[branch - 1]
        for i in (-1, 0, 1):
            g = 3 * (branch - 1) + i + 1
            tap = 1 + 3 * g
            w_wait(g)
            mask_at = (2 * (branch - 1) + (i + 1) // 2) * H

            if g == 0:
                def point(rb, carry):
                    at = pl.multiple_of(rb * px, 16)
                    y = dot(xs[3, pl.ds(pl.multiple_of(pn.hb * px + at, 16), px)], wbuf[0])
                    pbuf[0, rb // 2, lax.rem(rb, 2)] = y.astype(BF16)
                    return carry

                lax.fori_loop(0, MEMBERS, point, 0)
                first_stage(0).start()

            def block(rb, carry, step=step, i=i, tap=tap, mask_at=mask_at, branch=branch):
                at = pl.multiple_of(rb * px, 16)
                window = pl.ds(pl.multiple_of((rb + pn.hb + i * step) * px, 16), px)
                y = dot(xs[3 - branch, window], wbuf[tap])
                y = y + dot(xs[3, window], wbuf[tap + 1])
                y = y + dot(xs[3 + branch, window], wbuf[tap + 2])
                if i != 0:
                    y = jnp.concatenate(
                        [y[r * pn.S:(r + 1) * pn.S] * masks[mask_at + rb * pn.rpb + r] for r in range(pn.rpb)], axis=0
                    )
                if i > -1:
                    y = y + acc[pl.ds(at, px)]
                if i < 1:
                    acc[pl.ds(at, px)] = y
                else:
                    pbuf[branch, rb // 2, lax.rem(rb, 2)] = y.astype(BF16)
                return carry

            lax.fori_loop(0, MEMBERS, block, 0)
        first_stage(branch).start()
        middle(branch - 1)

    sums = dot(hot_t[...], xs[3, pl.ds(pn.hb * px, pn.own)])
    means = sums * inv_counts[...]
    m_out[...] = means
    p4_out[...] = split_dot(dot, means, wbuf[TAPS - 1])
    w_save = pltpu.make_async_copy(wbuf, w_out, o_s.at[1])
    w_save.start()
    middle(3)
    for slot in range(4):
        last(slot)

    @pl.when(to_up)
    def _():
        for kk in range(MEMBERS):
            halo(kk, False).wait_send()

    @pl.when(to_down)
    def _():
        for kk in range(MEMBERS):
            halo(kk, True).wait_send()

    if pn.exchange:
        for g in range(len(GROUPS)):
            for zz in range(1, pn.slabs):
                w_send(g, zz, col).wait_send()
    x_save.wait()
    w_save.wait()


def conv_forward(pn, feats, w, cot, masks, sel, hot_t, inv_counts):
    half = MEMBERS // 2
    dma = pltpu.SemaphoreType.DMA
    vmem = pl.BlockSpec(memory_space=pltpu.VMEM)
    hbm = pl.BlockSpec(memory_space=pl.ANY)
    shape = jax.ShapeDtypeStruct
    ng = len(GROUPS)
    return pl.pallas_call(
        functools.partial(conv_kernel, pn),
        out_shape=(
            shape((4, pn.px, pn.width), F32),
            shape((7, pn.ext, pn.cs), BF16),
            shape((TAPS, pn.cs, pn.width), BF16),
            shape((pn.ncp, pn.cs), F32),
            shape((pn.ncp, pn.width), F32),
            shape((pn.px, pn.width), BF16),
        ),
        in_specs=[hbm, hbm, hbm, pl.BlockSpec(memory_space=pltpu.SMEM), vmem, vmem, vmem],
        out_specs=(vmem, hbm, hbm, vmem, vmem, vmem),
        scratch_shapes=[
            pltpu.VMEM((pn.nb * pn.rpb, pn.C * pn.bp, pn.cs), BF16),
            pltpu.VMEM((7, pn.ext, pn.cs), BF16),
            pltpu.VMEM((TAPS, pn.cs, pn.width), BF16),
            pltpu.VMEM((pn.own, pn.width), F32),
            pltpu.VMEM((4, half, 2, pn.px, pn.width), BF16),
            pltpu.VMEM((4, half, pn.px, pn.width), BF16),
            pltpu.VMEM((4, half - 1, pn.px, pn.width), BF16),
            pltpu.VMEM((4, half - 1, pn.px, pn.width), BF16),
            pltpu.VMEM((pn.rpb, pn.C * pn.bp, pn.width), BF16),
            dma((MEMBERS,)), dma((MEMBERS,)), dma((2, MEMBERS)), dma((pn.C,)), dma((pn.C,)), dma((pn.C,)), dma((pn.C,)),
            dma((pn.C, ng)), dma((ng, pn.C)), dma((ng,)), dma((4,)), dma((4,)), dma((4, 3)), dma((4, 3)), dma((2,)),
        ],
        compiler_params=pltpu.CompilerParams(collective_id=0, has_side_effects=True, vmem_limit_bytes=60 * 2**20),
        name="conv_forward",
    )(feats, w, cot, masks, sel, hot_t, inv_counts)


def norm_kernel(pn, p, p4_in, gains, biases, valid, pixels, w_proj, cot, hot, hot_t, sel_t,
                q_out, q4_out, dproj_out, res_out, dg_out, db_out,
                norm, slope, hbuf, gact, dh4, rx,
                a1, b1, a2, b2, a3, b3, a4, b4, as_s, as_r, bs_s, bs_r, e_s, e_r):
    row, col = lax.axis_index("row"), lax.axis_index("col")
    slab, x = row // pn.G, lax.rem(row, pn.G)
    me = x * pn.C + col
    crops = float(pn.crops)
    v = valid[...]
    inv_px = pixels[0]
    width, bp = pn.width, pn.bp

    def member(s, k):
        return (s * pn.G + k // pn.C, lax.rem(k, pn.C))

    barrier = pltpu.get_barrier_semaphore()
    for kk in range(1, MEMBERS):
        pl.semaphore_signal(barrier, inc=1, device_id=member(slab, lax.rem(me + kk, MEMBERS)), device_id_type=MESH)

    def hello(k, carry):
        pl.semaphore_signal(barrier, inc=1, device_id=member(lax.rem(slab + k, pn.slabs), me), device_id_type=MESH)
        return carry

    lax.fori_loop(1, pn.slabs, hello, 0)

    def peer_a(n, abuf, kk):
        return remote(abuf.at[me], abuf.at[me], as_s.at[n, kk], as_r.at[n, kk], member(slab, lax.rem(me + kk, MEMBERS)))

    def peer_b(n, bbuf, k):
        return remote(bbuf.at[slab], bbuf.at[slab], bs_s.at[n, k], bs_r.at[n, k], member(lax.rem(slab + k, pn.slabs), me))

    def reduce_start(n, abuf):
        for kk in range(1, MEMBERS):
            peer_a(n, abuf, kk).start()

    def reduce_end(n, abuf, bbuf):
        for kk in range(1, MEMBERS):
            peer_a(n, abuf, kk).wait()
        total = abuf[0]
        for k in range(1, MEMBERS):
            total = total + abuf[k]
        bbuf[slab] = total
        for k in range(1, pn.slabs):
            peer_b(n, bbuf, k).start()
        for k in range(1, pn.slabs):
            peer_b(n, bbuf, k).wait()
        total = bbuf[0]
        for k in range(1, pn.slabs):
            total = total + bbuf[k]
        return total

    def column_sum(value):
        return jnp.sum(value, axis=0, keepdims=True)

    for b in range(4):
        pv = p[b] * v
        a1[me, pl.ds(b, 1)] = column_sum(pv)
        a1[me, pl.ds(4 + b, 1)] = column_sum(pv * p[b])
    a1[me, pl.ds(8, pn.ncp)] = p4_in[...]
    pl.semaphore_wait(barrier, MEMBERS - 1 + pn.slabs - 1)
    reduce_start(0, a1)
    total = reduce_end(0, a1, b1)
    inv = []
    for b in range(4):
        centre = total[b:b + 1] * inv_px
        scale = lax.rsqrt(total[4 + b:5 + b] * inv_px - centre * centre + EPSILON)
        inv.append(scale)
        n = (p[b] - centre) * scale
        u = gains[b:b + 1] * n + biases[b:b + 1]
        s = jax.nn.sigmoid(u)
        norm[b] = n
        slope[b] = s * (1.0 + u * (1.0 - s))
        hbuf[b] = (u * s).astype(BF16)
    p4 = total[8:8 + pn.ncp]
    centre4 = column_sum(p4) * (1.0 / crops)
    inv4 = lax.rsqrt(column_sum(p4 * p4) * (1.0 / crops) - centre4 * centre4 + EPSILON)
    n4 = (p4 - centre4) * inv4
    u4 = gains[4:5] * n4 + biases[4:5]
    s4 = jax.nn.sigmoid(u4)
    slope4 = s4 * (1.0 + u4 * (1.0 - s4))
    hbuf[4] = dot(hot[...], (u4 * s4).astype(BF16)).astype(BF16)

    p5 = dot(hbuf[0], w_proj[pl.ds(0, width)])
    for b in range(1, 5):
        p5 = p5 + dot(hbuf[b], w_proj[pl.ds(b * width, width)])
    pv = p5 * v
    a2[me, pl.ds(0, 1)] = column_sum(pv)
    a2[me, pl.ds(1, 1)] = column_sum(pv * p5)
    a2[me, pl.ds(2, 6)] = jnp.zeros((6, width), F32)
    reduce_start(1, a2)
    total = reduce_end(1, a2, b2)
    centre5 = total[0:1] * inv_px
    inv5 = lax.rsqrt(total[1:2] * inv_px - centre5 * centre5 + EPSILON)
    n5 = (p5 - centre5) * inv5
    u5 = gains[5:6] * n5 + biases[5:6]
    s5 = jax.nn.sigmoid(u5)
    g5 = cot[...].astype(F32) * v * (s5 * (1.0 + u5 * (1.0 - s5)))
    norm[4] = n5
    gact[4] = g5
    a3[me, pl.ds(0, 1)] = column_sum(g5)
    a3[me, pl.ds(1, 1)] = column_sum(g5 * n5)
    a3[me, pl.ds(2, 6)] = jnp.zeros((6, width), F32)
    reduce_start(2, a3)
    hbuf[5] = (v * u5 * s5).astype(BF16)
    for rp in range(pn.rpb // 2):
        pair = hbuf[5, pl.ds(rp * 2 * pn.S, 2 * pn.S)]
        rx[2 * rp:2 * rp + 2] = dot(sel_t[...], pair).astype(BF16).reshape(2, pn.C * bp, width)
    back = []
    for cc in range(1, pn.C):
        cd = lax.rem(col + cc, pn.C)
        c = remote(rx.at[:, pl.ds(pl.multiple_of(cd * bp, bp), bp)], res_out.at[pl.ds(col * pn.rpb, pn.rpb)],
                   e_s.at[cc], e_r.at[cc], (row, cd))
        c.start()
        back.append(c)
    c = pltpu.make_async_copy(rx.at[:, pl.ds(pl.multiple_of(col * bp, bp), bp)], res_out.at[pl.ds(col * pn.rpb, pn.rpb)],
                              e_r.at[0])
    c.start()
    back.append(c)
    total = reduce_end(2, a3, b3)
    db5, dg5 = total[0:1], total[1:2]
    q5 = (gains[5:6] * inv5 * (gact[4] - v * (db5 + norm[4] * dg5) * inv_px)).astype(BF16)
    hbuf[5] = q5

    for b in range(4):
        g = dot_nt(q5, w_proj[pl.ds(b * width, width)]) * slope[b]
        gact[b] = g
        a4[me, pl.ds(b, 1)] = column_sum(g)
        a4[me, pl.ds(4 + b, 1)] = column_sum(g * norm[b])
    dh4[...] = dot_nt(q5, w_proj[pl.ds(4 * width, width)])
    high = dh4[...].astype(BF16)
    low = (dh4[...] - high.astype(F32)).astype(BF16)
    a4[me, pl.ds(8, pn.ncp)] = dot(hot_t[...], high) + dot(hot_t[...], low)
    reduce_start(3, a4)
    for b in range(5):
        dproj_out[pl.ds(b * width, width)] = dot_tn(hbuf[b], hbuf[5]).astype(BF16)
    total = reduce_end(3, a4, b4)
    for b in range(4):
        db, dg = total[b:b + 1], total[4 + b:5 + b]
        db_out[pl.ds(b, 1)] = db
        dg_out[pl.ds(b, 1)] = dg
        q_out[b] = (gains[b:b + 1] * inv[b] * (gact[b] - v * (db + norm[b] * dg) * inv_px)).astype(BF16)
    g4 = total[8:8 + pn.ncp] * slope4
    db4, dg4 = column_sum(g4), column_sum(g4 * n4)
    db_out[pl.ds(4, 1)] = db4
    dg_out[pl.ds(4, 1)] = dg4
    db_out[pl.ds(5, 1)] = db5
    dg_out[pl.ds(5, 1)] = dg5
    q4_out[...] = (gains[4:5] * inv4 * (g4 - (db4 + n4 * dg4) * (1.0 / crops))).astype(BF16)
    for c in back:
        c.wait()


def norms(pn, p, p4, gains, biases, valid, pixels, w_proj, cot, hot, hot_t, sel_t):
    dma = pltpu.SemaphoreType.DMA
    vmem = pl.BlockSpec(memory_space=pltpu.VMEM)
    shape = jax.ShapeDtypeStruct
    big, small = 8 + pn.ncp, 8
    bufs = []
    for n in (big, small, small, big):
        bufs += [pltpu.VMEM((MEMBERS, n, pn.width), F32), pltpu.VMEM((pn.slabs, n, pn.width), F32)]
    return pl.pallas_call(
        functools.partial(norm_kernel, pn),
        out_shape=(
            shape((4, pn.px, pn.width), BF16),
            shape((pn.ncp, pn.width), BF16),
            shape((5 * pn.width, pn.width), BF16),
            shape((pn.h, pn.bp, pn.width), BF16),
            shape((6, pn.width), F32),
            shape((6, pn.width), F32),
        ),
        in_specs=[vmem] * 5 + [pl.BlockSpec(memory_space=pltpu.SMEM)] + [vmem] * 5,
        out_specs=(vmem,) * 6,
        scratch_shapes=[
            pltpu.VMEM((5, pn.px, pn.width), F32),
            pltpu.VMEM((4, pn.px, pn.width), F32),
            pltpu.VMEM((6, pn.px, pn.width), BF16),
            pltpu.VMEM((5, pn.px, pn.width), F32),
            pltpu.VMEM((pn.px, pn.width), F32),
            pltpu.VMEM((pn.rpb, pn.C * pn.bp, pn.width), BF16),
            *bufs,
            dma((4, MEMBERS)), dma((4, MEMBERS)), dma((4, pn.slabs)), dma((4, pn.slabs)), dma((pn.C,)), dma((pn.C,)),
        ],
        compiler_params=pltpu.CompilerParams(collective_id=1, has_side_effects=True, vmem_limit_bytes=48 * 2**20),
        name="norms",
    )(p, p4, gains, biases, valid, pixels, w_proj, cot, hot, hot_t, sel_t)


BACK = tuple((b, i) for b in (1, 2, 3) for i in (-1, 1)) + tuple((b, 0) for b in (1, 2, 3))


def back_kernel(pn, q_in, x_in, w_in, q4, means, hot_px, inv_counts, masks, lane_masks, shifts, sel_t,
                dw_out, dx_out,
                xs, wbuf, qraw, qs, qt, dxe, dwbuf, dwr, dwsum, hsend, hrecv, pack,
                l_s, q_s, q_r, k_s, k_r, f_s, f_r, d_s, d_r, g_s, g_r, h_s, h_r, x_s, x_r):
    row, col = lax.axis_index("row"), lax.axis_index("col")
    slab, x = row // pn.G, lax.rem(row, pn.G)
    me = x * pn.C + col
    core, quad = lax.rem(col, 2), me // 2
    h, H, bp, px, S = pn.h, pn.H, pn.bp, pn.px, pn.S
    half = MEMBERS // 2
    partner = (row, col + 1 - 2 * core)

    def member(s, k):
        return (s * pn.G + k // pn.C, lax.rem(k, pn.C))

    load_x = pltpu.make_async_copy(x_in, xs, l_s.at[0])
    load_w = pltpu.make_async_copy(w_in, wbuf, l_s.at[1])
    load_x.start()
    load_w.start()
    greet_all(pn, row, col)

    def straight(slot, i):
        other = 2 * lax.rem(quad + i, half) + core
        return remote(q_in.at[slot], qraw.at[slot, pl.ds(pl.multiple_of(me * px, 16), px)], q_s.at[slot, i], q_r.at[slot, i],
                      member(slab, other))

    def to_partner(slot):
        return remote(q_in.at[slot], qraw.at[slot, pl.ds(pl.multiple_of(me * px, 16), px)], k_s.at[slot], k_r.at[slot], partner)

    def passed(slot, i):
        origin = 2 * lax.rem(quad - i + half, half) + core
        at = pl.ds(pl.multiple_of(origin * px, 16), px)
        return remote(qraw.at[slot, at], qraw.at[slot, at], f_s.at[slot, i], f_r.at[slot, i], partner)

    slots = (1, 2, 3, 0)
    for slot in slots:
        for i in range(1, half):
            straight(slot, i).start()
        to_partner(slot).start()
    own_q = []
    for slot in slots:
        c = pltpu.make_async_copy(q_in.at[slot], qraw.at[slot, pl.ds(pl.multiple_of(me * px, 16), px)], l_s.at[2 + slot])
        c.start()
        own_q.append(c)

    def clear(rb, carry):
        dxe[pl.ds(pl.multiple_of(rb * px, 16), px)] = jnp.zeros((px, pn.cs), F32)
        return carry

    lax.fori_loop(0, pn.nb, clear, 0)

    def receive(slot):
        for i in range(1, half):
            straight(slot, i).wait()
            passed(slot, i).start()

    def received(slot):
        to_partner(slot).wait()
        own_q[slots.index(slot)].wait()
        for i in range(1, half):
            passed(slot, i).wait()

    def out_piece(n, jj):
        taps = back_taps(n)
        j = lax.rem(col + jj, pn.C)
        src = dwbuf.at[pl.ds(taps[0], len(taps)), pl.ds(pl.multiple_of(j * pn.part, pn.part), pn.part)]
        dst = dwr.at[slab, pl.ds(taps[0], len(taps))]
        return src, dst, (col * pn.G + x, j)

    def send_piece(n):
        if not pn.exchange:
            return
        for jj in range(1, pn.C):
            src, dst, to = out_piece(n, jj)
            remote(src, dst, d_s.at[n, jj], d_r.at[n, slab], to).start()
        src, dst, to = out_piece(n, 0)

        @pl.when(slab == col)
        def _():
            pltpu.make_async_copy(src, dst, d_r.at[n, slab]).start()

        @pl.when(slab != col)
        def _():
            remote(src, dst, d_s.at[n, 0], d_r.at[n, slab], to).start()

    def piece_sent(n):
        for jj in range(1, pn.C):
            src, dst, to = out_piece(n, jj)
            remote(src, dst, d_s.at[n, jj], d_r.at[n, slab], to).wait_send()
        src, dst, to = out_piece(n, 0)

        @pl.when(slab != col)
        def _():
            remote(src, dst, d_s.at[n, 0], d_r.at[n, slab], to).wait_send()

    def back_taps(n):
        if n < len(BACK):
            b, i = BACK[n]
            first = 1 + 9 * (b - 1) + 3 * (i + 1)
            return (first, first + 1, first + 2)
        return (0,) if n == len(BACK) else (TAPS - 1,)

    load_x.wait()
    load_w.wait()
    receive(1)
    for n, (branch, i) in enumerate(BACK):
        step = pn.steps[branch - 1]
        taps = back_taps(n)
        if i == -1:
            received(branch)
            if branch < 3:
                receive(branch + 1)
            else:
                receive(0)

            def turn(rp, carry, branch=branch):
                at = pl.multiple_of(rp * 2 * S, 16)
                moved = dot(shifts[pl.ds((branch - 1) * 4 * S, 4 * S)], qraw[branch, pl.ds(at, 2 * S)]).astype(BF16)
                qs[branch - 1, 0, pl.ds(at, 2 * S)] = moved[:2 * S]
                qs[branch - 1, 1, pl.ds(at, 2 * S)] = moved[2 * S:]
                return carry

            lax.fori_loop(0, H // 2, turn, 0)
            qt[branch] = qraw[branch].T

        q_turned = qt[branch]
        if i != 0:
            q_turned = q_turned * lane_masks[pl.ds(2 * (branch - 1) + (i + 1) // 2, 1)]
        window = pl.ds((pn.hb + i * step) * px, pn.own)
        for j, tap in zip((-1, 0, 1), taps):
            dwbuf[tap] = dot(q_turned, xs[3 + j * branch, window]).T.astype(BF16)
        send_piece(n)
        mask_at = (2 * (branch - 1) + (i + 1) // 2) * H

        def block(rb, carry, branch=branch, i=i, step=step, taps=taps, mask_at=mask_at):
            at = pl.ds(pl.multiple_of(rb * px, 16), px)
            y = dot_nt(qs[branch - 1, 0, at], wbuf[taps[0]])
            y = y + dot_nt(qraw[branch, at], wbuf[taps[1]])
            y = y + dot_nt(qs[branch - 1, 1, at], wbuf[taps[2]])
            if i != 0:
                y = jnp.concatenate([y[r * S:(r + 1) * S] * masks[mask_at + rb * pn.rpb + r] for r in range(pn.rpb)], axis=0)
            to = pl.ds(pl.multiple_of((rb + pn.hb + i * step) * px, 16), px)
            dxe[to] = dxe[to] + y
            return carry

        lax.fori_loop(0, MEMBERS, block, 0)
        if n == 5:
            hsend[0] = dxe[pl.ds(0, pn.hb * px)].astype(BF16)
            hsend[1] = dxe[pl.ds((pn.hb + MEMBERS) * px, pn.hb * px)].astype(BF16)

            @pl.when(slab > 0)
            def _():
                remote(hsend.at[0], hrecv.at[1], h_s.at[0], h_r.at[1], member(slab - 1, me)).start()

            @pl.when(slab < pn.slabs - 1)
            def _():
                remote(hsend.at[1], hrecv.at[0], h_s.at[1], h_r.at[0], member(slab + 1, me)).start()

    received(0)
    n_point, n_pool = len(BACK), len(BACK) + 1
    dwbuf[TAPS - 1] = dot_tn(means[...].astype(BF16), q4[...]).astype(BF16)
    dwbuf[0] = dot(qraw[0].T, xs[3, pl.ds(pn.hb * px, pn.own)]).T.astype(BF16)
    send_piece(n_point)
    send_piece(n_pool)
    pooled = dot_nt(q4[...], wbuf[TAPS - 1]) * inv_counts[...]
    pooled_high = pooled.astype(BF16)
    pooled_low = (pooled - pooled_high.astype(F32)).astype(BF16)

    @pl.when(slab > 0)
    def _():
        remote(hsend.at[0], hrecv.at[1], h_s.at[0], h_r.at[1], member(slab - 1, me)).wait_send()
        remote(hsend.at[1], hrecv.at[0], h_s.at[1], h_r.at[0], member(slab - 1, me)).wait_recv()

    @pl.when(slab < pn.slabs - 1)
    def _():
        remote(hsend.at[1], hrecv.at[0], h_s.at[1], h_r.at[0], member(slab + 1, me)).wait_send()
        remote(hsend.at[0], hrecv.at[1], h_s.at[0], h_r.at[1], member(slab + 1, me)).wait_recv()

    @pl.when(slab == 0)
    def _():
        hrecv[0] = jnp.zeros((pn.hb * px, pn.cs), BF16)

    @pl.when(slab == pn.slabs - 1)
    def _():
        hrecv[1] = jnp.zeros((pn.hb * px, pn.cs), BF16)

    def finish(rb, carry):
        at = pl.ds(pl.multiple_of(rb * px, 16), px)
        y = dxe[pl.ds(pl.multiple_of((rb + pn.hb) * px, 16), px)] + dot_nt(qraw[0, at], wbuf[0])
        hot = hot_px[at]
        y = y + dot(hot, pooled_high) + dot(hot, pooled_low)
        dxe[pl.ds(pl.multiple_of((rb + pn.hb) * px, 16), px)] = y
        return carry

    lax.fori_loop(0, MEMBERS, finish, 0)
    for rb in range(pn.hb):
        low, high = (pn.hb + rb) * px, (MEMBERS + rb) * px
        dxe[pl.ds(low, px)] = dxe[pl.ds(low, px)] + hrecv[0, pl.ds(rb * px, px)].astype(F32)
        dxe[pl.ds(high, px)] = dxe[pl.ds(high, px)] + hrecv[1, pl.ds(rb * px, px)].astype(F32)

    def packing(rp, carry):
        pair = dxe[pl.ds(pl.multiple_of(pn.hb * px + rp * 2 * S, 16), 2 * S)].astype(BF16)
        pack[pl.ds(2 * rp, 2)] = dot(sel_t[...], pair).astype(BF16).reshape(2, pn.C * bp, pn.cs)
        return carry

    lax.fori_loop(0, H // 2, packing, 0)
    home = []
    for kk in range(1, MEMBERS):
        other = lax.rem(me + kk, MEMBERS)
        xo, co = other // pn.C, lax.rem(other, pn.C)
        c = remote(pack.at[pl.ds(xo * h, h), pl.ds(pl.multiple_of(co * bp, bp), bp)], dx_out.at[me], x_s.at[kk], x_r.at[kk],
                   member(slab, other))
        c.start()
        home.append(c)
    c = pltpu.make_async_copy(pack.at[pl.ds(x * h, h), pl.ds(pl.multiple_of(col * bp, bp), bp)], dx_out.at[me], x_r.at[0])
    c.start()
    home.append(c)

    own_part = pl.ds(pl.multiple_of(col * pn.part, pn.part), pn.part)

    def share(n, jj):
        taps = back_taps(n)
        t = pl.ds(taps[0], len(taps))
        return remote(dwsum.at[t], dw_out.at[t, own_part], g_s.at[n, jj], g_r.at[n, jj], (row, lax.rem(col + jj, pn.C)))

    def share_own(n):
        taps = back_taps(n)
        t = pl.ds(taps[0], len(taps))
        return pltpu.make_async_copy(dwsum.at[t], dw_out.at[t, own_part], g_r.at[n, 0])

    pieces = len(BACK) + 2
    if pn.exchange:
        for n in range(pieces):
            taps = back_taps(n)
            t = pl.ds(taps[0], len(taps))
            for z in range(pn.slabs):
                pltpu.make_async_copy(dwr.at[z, t], dwr.at[z, t], d_r.at[n, z]).wait()
            for tap in taps:
                total = dwr[0, tap].astype(F32)
                for z in range(1, pn.slabs):
                    total = total + dwr[z, tap].astype(F32)
                dwsum[tap] = total.astype(BF16)
            for jj in range(1, pn.C):
                share(n, jj).start()
            share_own(n).start()
        for n in range(pieces):
            piece_sent(n)
            for jj in range(1, pn.C):
                share(n, jj).wait()
            share_own(n).wait()
    else:
        c = pltpu.make_async_copy(dwbuf, dw_out, g_r.at[0, 0])
        c.start()
        c.wait()
    for c in home:
        c.wait()


def conv_backward(pn, q, xs, w, q4, means, hot_px, inv_counts, masks, lane_masks, shifts, sel_t):
    dma = pltpu.SemaphoreType.DMA
    vmem = pl.BlockSpec(memory_space=pltpu.VMEM)
    hbm = pl.BlockSpec(memory_space=pl.ANY)
    shape = jax.ShapeDtypeStruct
    half = MEMBERS // 2
    pieces = len(BACK) + 2
    return pl.pallas_call(
        functools.partial(back_kernel, pn),
        out_shape=(
            shape((TAPS, pn.cs, pn.width), BF16),
            shape((MEMBERS, pn.h, pn.bp, pn.cs), BF16),
        ),
        in_specs=[hbm, hbm, hbm, vmem, vmem, vmem, vmem, pl.BlockSpec(memory_space=pltpu.SMEM), vmem, vmem, vmem],
        out_specs=(hbm, hbm),
        scratch_shapes=[
            pltpu.VMEM((7, pn.ext, pn.cs), BF16),
            pltpu.VMEM((TAPS, pn.cs, pn.width), BF16),
            pltpu.VMEM((4, pn.own, pn.width), BF16),
            pltpu.VMEM((3, 2, pn.own, pn.width), BF16),
            pltpu.VMEM((4, pn.width, pn.own), BF16),
            pltpu.VMEM((pn.ext, pn.cs), F32),
            pltpu.VMEM((TAPS, pn.cs, pn.width), BF16),
            pltpu.VMEM((pn.C, TAPS, pn.part, pn.width), BF16),
            pltpu.VMEM((TAPS, pn.part, pn.width), BF16),
            pltpu.VMEM((2, pn.hb * pn.px, pn.cs), BF16),
            pltpu.VMEM((2, pn.hb * pn.px, pn.cs), BF16),
            pltpu.VMEM((pn.H, pn.C * pn.bp, pn.cs), BF16),
            dma((6,)), dma((4, half)), dma((4, half)), dma((4,)), dma((4,)), dma((4, half)), dma((4, half)),
            dma((pieces, pn.C)), dma((pieces, pn.C)), dma((pieces, pn.C)), dma((pieces, pn.C)),
            dma((2,)), dma((2,)), dma((MEMBERS,)), dma((MEMBERS,)),
        ],
        compiler_params=pltpu.CompilerParams(collective_id=2, has_side_effects=True, vmem_limit_bytes=61 * 2**20),
        name="conv_backward",
    )(q, xs, w, q4, means, hot_px, inv_counts, masks, lane_masks, shifts, sel_t)


def column_tables(pn):
    S, bp, bc = pn.S, pn.bp, pn.bc
    sel = np.zeros((7, 2, S, 2, pn.C * bp), np.float32)
    shifts = np.zeros((3, 2, 2, S, 2, S), np.float32)
    for r in range(2):
        for c in range(pn.cols):
            for v in range(-3, 4):
                s = c + v * DILATIONS[0]
                if 0 <= s < pn.cols:
                    sel[v + 3, r, c, r, (s // bc) * bp + s % bc] = 1.0
            for b, d in enumerate(DILATIONS):
                for n, j in enumerate((-1, 1)):
                    s = c - j * d
                    if 0 <= s < pn.cols:
                        shifts[b, n, r, c, r, s] = 1.0
    sel = sel.reshape(7 * 2 * S, 2 * pn.C * bp)
    sel_t = sel[3 * 2 * S:4 * 2 * S].T
    return (jnp.asarray(sel, BF16), jnp.asarray(sel_t, BF16), jnp.asarray(shifts.reshape(12 * S, 2 * S), BF16))


def per_device(
    features, crop_rows, crop_cols, w_point, w_atrous, w_pool, w_proj, gains, biases, cotangent
):
    h, bc, channels = features.shape
    pn = Plan(lax.axis_size("row"), lax.axis_size("col"), h, bc, channels, gains.shape[1], crop_rows.shape[0])
    row, col = lax.axis_index("row"), lax.axis_index("col")
    slab, x = row // pn.G, row % pn.G
    crop_ids = jnp.arange(pn.crops, dtype=jnp.int32)
    ends = jnp.cumsum(crop_rows)
    counts = (crop_rows * crop_cols).astype(F32)
    pixels = jnp.sum(counts)

    def crop_of(rows):
        found = jnp.sum((rows[:, None] >= ends[None, :]).astype(jnp.int32), axis=1)
        return jnp.where(rows < 0, -1, found)

    def widths_of(crop):
        return jnp.sum(jnp.where(crop[:, None] == crop_ids[None, :], crop_cols[None, :], 0), axis=1)

    own_crop = crop_of(row * h + jnp.arange(h, dtype=jnp.int32))
    own_columns = col * bc + jnp.arange(bc, dtype=jnp.int32)
    own_valid = own_columns[None, :] < widths_of(own_crop)[:, None]
    masked = jnp.where(own_valid[:, :, None], features, 0)
    feats = masked.reshape(h, bc, pn.C, pn.G, pn.cs).transpose(3, 2, 0, 1, 4).reshape(MEMBERS, h, bc, pn.cs)
    feats = jnp.pad(feats, ((0, 0), (0, 0), (0, pn.bp - bc), (0, 0)))
    cot = jnp.pad(cotangent, ((0, 0), (0, pn.bp - bc), (0, 0)))

    slab_rows = slab * pn.H - MARGIN + jnp.arange(pn.H + 2 * MARGIN, dtype=jnp.int32)
    crops = crop_of(slab_rows)
    mid = crops[MARGIN:MARGIN + pn.H]
    same = jnp.stack(
        [crops[MARGIN + i * d:MARGIN + i * d + pn.H] == mid for d in DILATIONS for i in (-1, 1)]
    ).astype(F32)
    lane_masks = jnp.pad(jnp.repeat(same, pn.S, axis=1), ((0, 2), (0, 0))).astype(BF16)
    ncp_ids = jnp.arange(pn.ncp, dtype=jnp.int32)
    hot_rows = (mid[:, None] == ncp_ids[None, :]).astype(BF16)
    hot_px = jnp.repeat(hot_rows, pn.S, axis=0)
    hot_t = jnp.repeat(hot_rows.T, pn.S, axis=1)
    inv_counts = jnp.pad(1.0 / counts, (0, pn.ncp - pn.crops))[:, None]

    k = x * pn.C + col
    block_crop = lax.dynamic_slice_in_dim(mid, k * pn.rpb, pn.rpb)
    columns = jnp.arange(pn.S, dtype=jnp.int32)
    valid = (columns[None, :] < widths_of(block_crop)[:, None]).astype(F32).reshape(pn.px, 1)
    block_hot = jnp.repeat((block_crop[:, None] == ncp_ids[None, :]).astype(BF16), pn.S, axis=0)
    block_hot_t = jnp.repeat((ncp_ids[:, None] == block_crop[None, :]).astype(BF16), pn.S, axis=1)

    sel, sel_t, shifts = column_tables(pn)
    w = jnp.concatenate([w_point[None], w_atrous.transpose(1, 0, 2), w_pool[None]], axis=0)
    full_proj = lax.all_gather(w_proj, "row", axis=0, tiled=True)
    if not pn.exchange:
        w = lax.all_gather(w, "row", axis=1, tiled=True)
        w = lax.dynamic_slice_in_dim(w, (col * pn.G + x) * pn.cs, pn.cs, axis=1)
    flat = same.reshape(-1)
    p, xs, w_own, means, p4, own_cot = conv_forward(pn, feats, w, cot, flat, sel, hot_t, inv_counts)
    q, q4, d_proj, res, d_gains, d_biases = norms(
        pn, p, p4, gains, biases, valid, (1.0 / pixels)[None], full_proj, own_cot, block_hot, block_hot_t, sel_t
    )
    dw, dx = conv_backward(pn, q, xs, w_own, q4, means, hot_px, inv_counts, flat, lane_masks, shifts, sel_t)
    if not pn.exchange:
        whole = jnp.zeros((TAPS, channels, pn.width), BF16)
        whole = lax.dynamic_update_slice(whole, dw, (0, (col * pn.G + x) * pn.cs, 0))
        whole = lax.psum(whole, "col")
        dw = lax.psum_scatter(whole, "row", scatter_dimension=1, tiled=True)
    d_proj = lax.psum(d_proj, "col")
    d_proj = lax.psum_scatter(d_proj.astype(F32), "row", scatter_dimension=0, tiled=True)
    result = res[:, :bc]
    dx = dx[:, :, :bc].reshape(pn.G, pn.C, h, bc, pn.cs).transpose(2, 3, 1, 0, 4).reshape(h, bc, channels)
    d_features = jnp.where(own_valid[:, :, None], dx, 0)
    d_point = dw[0].astype(F32)
    d_atrous = dw[1:TAPS - 1].astype(F32).transpose(1, 0, 2)
    d_pool = dw[TAPS - 1].astype(F32)
    return (result, d_features, d_point, d_atrous, d_pool, d_proj, d_gains, d_biases)


def solution(mesh):
    return jax.shard_map(
        per_device,
        mesh=mesh,
        in_specs=(
            P("row", "col", None),
            P(),
            P(),
            P("row", None),
            P("row", None, None),
            P("row", None),
            P("row", None),
            P(),
            P(),
            P("row", "col", None),
        ),
        out_specs=(
            P("row", "col", None),
            P("row", "col", None),
            P("row", None),
            P("row", None, None),
            P("row", None),
            P("row", None),
            P(),
            P(),
        ),
        check_vma=False,
    )
```

time: 2670 us -> 557 us (0.21)
  waiting for transfers between devices: 1900 us -> 32.9 us
  Pallas kernels: 0 us -> 443 us
  local copies, waits for them, and re-layouts: 304 us -> 18.7 us
  matrix products: 178 us -> 0 us
  blocking collectives: 186 us -> 23.9 us
  other arithmetic: 59 us -> 20.4 us
    reduce_scatter x4 -> x1, waiting for transfers between devices: 1030 us -> 0.01 us  [per_device(): lax.psum_scatter(d_proj.astype(F32), 'row', scatter_dimension=0, tiled=True)]
    all_gather x4 -> x0, waiting for transfers between devices: 596 us -> none  [the longest x1 539 us: per_device(): lax.all_gather(w_atrous, 'row', axis=0, tiled=True)]
    pallas_call x0 -> x3, Pallas kernels: none -> 443 us  [the longest x1 253 us: conv_backward(): pl.pallas_call(functools.partial(back_kernel, pn), out_shape=(shape((TAPS...]
    dynamic_update_slice x21 -> x0, local copies, waits for them, and re-layouts: 216 us -> none  [per_device(): lax.dynamic_update_slice(grad_extended, current + update, corner)]
    dot_general x95 -> x0, matrix products: 178 us -> none  [the longest x27 84.5 us: per_device(): jnp.einsum('rco,fo->rcf', masked_grad, full_atrous[:, tap_index, :], pref...]
    psum x4 -> x0, blocking collectives: 160 us -> none  [the longest x1 40.9 us: per_device(): lax.psum((local_bias, local_gain, crop_grad), ('row', 'col'))]
    psum x1, waiting for transfers between devices: 171 us -> 32.9 us  [per_device(): d_proj = lax.psum(d_proj, 'col')]
    ppermute x4 -> x0, waiting for transfers between devices: 105 us -> none  [the longest x2 99.4 us: padded_2(): before = lax.ppermute(last, axis, up)]
  transfers between devices with their start and end apart: 13 -> 2, of which waited for: 10 -> 1; matrix products, arithmetic and copies ran while one was open for 17% -> 3% of each run, Pallas kernels for 0% -> 46%
where the time goes in v1:
time: 557 us; the launch traced here: 554 us
  Pallas kernels  443 us (80%)
  waiting for transfers between devices  32.9 us (6%)
  blocking collectives  23.9 us (4%)
  other arithmetic  20.4 us (4%)
  local copies, waits for them, and re-layouts  18.7 us (3%)
  between operations  14.9 us (3%)
    pallas_call x1, Pallas kernels, conv_backward(): pl.pallas_call(functools.partial(back_kernel, pn), out_shape=(shape((TAPS...  253 us
    pallas_call x1, Pallas kernels, conv_forward(): pl.pallas_call(functools.partial(conv_kernel, pn), out_shape=(shape((4, p...  150 us
    pallas_call x1, Pallas kernels, norms(): pl.pallas_call(functools.partial(norm_kernel, pn), out_shape=(shape((4, p...  40.1 us
    psum x1, waiting for transfers between devices, per_device(): d_proj = lax.psum(d_proj, 'col')  32.9 us
    all_gather x1, blocking collectives, per_device(): full_proj = lax.all_gather(w_proj, 'row', axis=0, tiled=True)  23.9 us
  transfers between devices with their start and end apart: 2, of which 1 were waited for; matrix products, arithmetic and copies ran while one was open for 3% of the time, Pallas kernels for 46%

profile of v1, /device:TPU:9, one launch (start us, length us, event | category | flops | bytes accessed | tf_op | source)
XLA Modules:
  0.0 553.9 jit_solution(450512533224891316)
XLA Ops:
  7.2 0.8 reduce-window.8
  8.1 0.1 convert_reduce_fusion
  8.2 0.1 compare_bitcast_fusion
  8.2 0.1 slice.37
  8.3 1.3 convert_reduce_fusion.2
  9.6 0.1 dynamic_slice.3
  9.7 0.8 select_reduce_fusion
  10.6 0.1 convert_reduce_fusion.1
  10.7 0.7 select_reduce_fusion.1
  11.4 0.1 broadcast_compare_fusion
  11.5 1.5 broadcast_select_fusion.1
  13.0 0.9 reshape.157
  13.9 0.7 copy.34
  14.6 0.2 copy-done.8
  14.8 1.4 pad.17.feats
  16.2 0.7 pad.18.cot
  17.0 0.7 reshape.166.masks
  17.6 0.2 broadcast_in_dim.105
  17.8 0.9 reshape.159.hot_t
  18.7 0.7 copy.36.inv_counts
  19.4 0.1 reshape.170.valid
  19.6 23.9 %all_gather.3.w_proj = bf16[1280,256]{1,0:T(8,128)(2,1)S(1)} all-gather(bf16[160,256]{1,0:T(8,128)(2,1)S(1)} %copy-done.11), channel_id=1, replica_groups=mesh['row'=8,'col'=4] {'row'}, dimensions={0}, use_global_device_ids=true | all-gather | bytes 737280 | tf_op jit(solution)/shard_map/all_gather | solution.py:907
  43.5 0.1 broadcast_in_dim.111
  43.6 0.1 reshape.161.hot_t
  44.4 3.6 pad_maximum_fusion.w_in
  48.0 150.3 %conv_forward.1 = (f32[4,336,256]{2,1,0:T(8,128)}, bf16[7,4704,256]{2,1,0:T(8,128)(2,1)}, bf16[29,256,256]{2,1,0:T(8,128)(2,1)}, f32[16,256]{1,0:T(8,128)}, f32[16,256]{1,0:T(8,128)}, /*index=5*/bf16[336,256]{1,0:T(8,128)(2,1)}) custom-call(bf16[8,24,16,256]{3,2,1,0:T(8,128)(2,1)} %pad.17.feats, bf16[29,256,256]{2,1,0:T(8,128)(2,1)} %pad_maximum_fusion.w_in, ...), custom_call_target="tpu_custom_call" | custom-call | tf_op jit(solution)/shard_map/conv_forward/pallas_call | solution.py:323
  198.4 1.3 copy-done
  199.8 0.9 copy-done.2
  200.7 0.7 copy-done.4
  201.4 40.1 %norms.1 = (bf16[4,336,256]{2,1,0:T(8,128)(2,1)S(1)}, bf16[16,256]{1,0:T(8,128)(2,1)S(1)}, bf16[1280,256]{1,0:T(8,128)(2,1)}, bf16[24,16,256]{2,1,0:T(8,128)(2,1...) custom-call(f32[4,336,256]{2,1,0:T(8,128)S(1)} %copy-done, f32[16,256]{1,0:T(8,128)S(1)} %copy-done.4, ...), custom_call_target="tpu_custom_call" | custom-call | tf_op jit(solution)/shard_map/norms/pallas_call | solution.py:513
  241.5 0.8 copy-done.1
  242.3 0.6 copy-done.7
  243.0 32.9 %all-reduce.6.cloned.1.call-done = bf16[1280,256]{1,0:T(8,128)(2,1)} async-done(((bf16[1280,256]{1,0:T(8,128)(2,1)}), bf16[1280,256]{1,0:T(8,128)(2,1)}) %all-reduce.6.cloned.1.call-update) | async-done | bytes 655376 | tf_op jit(solution)/shard_map/psum | solution.py:922
  275.9 2.2 convert_element_type.87
  278.1 0.7 copy.40
  278.8 0.1 broadcast_in_dim.113
  278.9 0.2 reshape.163
  279.1 0.6 pad.20.lane_masks
  279.7 0.1 fusion
  279.8 0.9 broadcast_in_dim.112
  280.8 252.6 %conv_backward.1 = (bf16[29,256,256]{2,1,0:T(8,128)(2,1)}, bf16[8,24,16,256]{3,2,1,0:T(8,128)(2,1)}) custom-call(bf16[4,336,256]{2,1,0:T(8,128)(2,1)} %copy-done.1, bf16[7,4704,256]{2,1,0:T(8,128)(2,1)} %get-tuple-element.27.x_in, bf16[29,256,256]{2,1,0:T(8,128)(2,1)} %get-tuple-element.28.w_in, bf16[16,256]{1,0:T(8,128)(2,1)} %copy-done.7, ...), custom_call_target="tpu_custom_call" | custom-call | tf_op jit(solution)/shard_map/conv_backward/pallas_call | solution.py:808
  533.3 2.8 copy.39
  536.1 0.9 reshape.165
  537.1 1.8 bitcast_convert_fusion
  538.9 5.8 %convert_bitcast_fusion = f32[256,27,256]{2,0,1:T(8,128)} fusion(bf16[29,256,256]{2,1,0:T(8,128)(2,1)} %get-tuple-element.32), kind=kLoop, calls=%fused_computation | loop fusion | flops 1769472 | bytes 10616832 | tf_op jit(solution)/shard_map/transpose | solution.py:928
  544.7 1.2 broadcast_select_fusion
  545.9 0.6 copy.44
  546.5 0.6 copy.45
  (37 shorter events, 0.4 us)
Async XLA Ops:
  7.2 268.7 %all-reduce.6.cloned.1.call-start = ((), (), s32[]{:S(2)}) async-start(), calls=%async_computation.1 | async-start | bytes 1310720 | tf_op jit(solution)/shard_map/psum | solution.py:922
  13.9 0.9 copy-start.8
  14.8 4.7 copy-start.11
  16.2 28.2 %copy-start.9 = (bf16[256,256]{1,0:T(8,128)(2,1)S(1)}, bf16[256,256]{1,0:T(8,128)(2,1)}, u32[]{:S(2)}) copy-start(bf16[256,256]{1,0:T(8,128)(2,1)} %param.18) | copy-start | bytes 393220
  16.2 28.2 %copy-start.10 = (bf16[256,256]{1,0:T(8,128)(2,1)S(1)}, bf16[256,256]{1,0:T(8,128)(2,1)}, u32[]{:S(2)}) copy-start(bf16[256,256]{1,0:T(8,128)(2,1)} %param.16) | copy-start | bytes 393220
  48.0 150.4 %copy-start.3 = (bf16[128,112]{1,0:T(8,128)(2,1)S(1)}, bf16[128,112]{1,0:T(8,128)(2,1)}, u32[]{:S(2)}) copy-start(bf16[128,112]{1,0:T(8,128)(2,1)} %constant.69.clone.sel_t) | copy-start | bytes 86020
  48.0 150.4 %copy-start.5 = (f32[6,256]{1,0:T(8,128)S(1)}, f32[6,256]{1,0:T(8,128)}, u32[]{:S(2)}) copy-start(f32[6,256]{1,0:T(8,128)} %gains.1) | copy-start | bytes 18436
  48.0 150.4 %copy-start.6 = (f32[6,256]{1,0:T(8,128)S(1)}, f32[6,256]{1,0:T(8,128)}, u32[]{:S(2)}) copy-start(f32[6,256]{1,0:T(8,128)} %biases.1) | copy-start | bytes 18436
  198.4 1.3 copy-start
  199.8 0.9 copy-start.2
  200.7 0.7 copy-start.4
  241.5 0.8 copy-start.1
  242.3 0.6 copy-start.7
  243.0 302.9 %reduce-scatter.2.cloned.1.call-start = ((), (), s32[]{:S(2)}) async-start(), calls=%async_computation.2 | async-start | bytes 1474560 | tf_op jit(solution)/shard_map/reduce_scatter | solution.py:923
Sparse Core Ops, SparseCore 0:
  243.1 32.7 all-reduce.5
  279.8 94.3 reduce-scatter.1
